TPU v7x, 1024 devices: a whole 4x8x16 slice. The times are simulated.
1024 devices in a mesh: enc: 64 (over y, x, core), pb: 16 (over z).
Axes of the slice: x: 4, y: 8, z: 16, core: 2. Of those that a mesh axis runs over, the one named last changes fastest.
Arguments:
- queries: bfloat16 [64, 3072, 4096], P('enc', 'pb'), as said below
- passages: bfloat16 [64, 128, 4096], P('enc', 'pb'), as said below
- table: bfloat16 [16, 2048, 2, 4096], P('pb', 'enc'), may hold values from -0.09375 to 0.09375
- neg_blocks: int32 [64, 3072, 16], P('enc', 'pb'), may hold values from 0 to 2047, as said below
- block_lists: int32 [64, 16, 64, 1], P('enc', 'pb'), may hold values from 0 to 31, as said below
- block_counts: int32 [64, 16, 64], P('enc', 'pb'), may hold values from 0 to 1, as said below
- pos_index: int32 [64, 3072], P('enc', 'pb'), may hold values from 0 to 127
Outputs:
- losses: float32 [64, 3072], P('enc', 'pb')
- passage_grads: float32 [64, 128, 4096], P('enc', 'pb')
- table_grads: float32 [16, 2048, 2, 4096], P('pb', 'enc')
Inputs may be any that keep to these rules, and one draw needn't show every extreme that they name: `queries`: entries lie within the stated range. `passages`: entries lie within the stated range. `neg_blocks`: the 16 ids of a query name blocks of 16 different owners (owner = id // 32); for owner o the id is o * 32 + block_lists[e, p, o, c] for some c < block_counts[e, p, o] of the query's device. `block_lists`: the 1 entries of one device and one owner are different blocks. `block_counts`: each count is 0 or 1; for every device all but 64 // 4 owners have 1.
All inputs are finite; a program needn't handle non-finite values.
Results may differ from a plain program's by a relative error of at most 0.015.
Values may be sent and summed in bfloat16 or wider, within the bound.
A program may use at most 32 MiB of HBM per device.

v0:
```python
import jax
import jax.numpy as jnp
from jax import lax
from jax.sharding import PartitionSpec as P

score_scale = 50.0


def body(queries, passages, table, neg_blocks, block_lists, block_counts, pos_index):
    owner_count = lax.axis_size("enc")
    query_rows = queries[0]
    query_count = query_rows.shape[0]
    local_blocks = table.shape[1]
    block_rows = table.shape[2]
    feature_width = table.shape[3]
    slot_count = block_lists.shape[3]
    labels = pos_index[0]
    asked = lax.all_to_all(block_lists[0, 0], "enc", split_axis=0, concat_axis=0, tiled=True)
    chosen = jnp.take(table[0], asked.reshape(-1), axis=0)
    chosen = chosen.reshape(asked.shape + (block_rows, feature_width))
    fetched = lax.all_to_all(chosen, "enc", split_axis=0, concat_axis=0, tiled=True)
    hard_rows = fetched.reshape(-1, feature_width)
    hard_logits = (
        jnp.einsum("qd,rd->qr", query_rows, hard_rows, preferred_element_type=jnp.float32)
        * score_scale
    )
    owner_ids = jnp.arange(owner_count, dtype=jnp.int32)
    named_owner = jnp.any(
        (neg_blocks[0] // local_blocks)[:, :, None] == owner_ids[None, None, :], axis=1
    )
    usable_slot = jnp.arange(slot_count, dtype=jnp.int32)[None, :] < block_counts[0, 0][:, None]
    live_mask = named_owner[:, :, None, None] & usable_slot[None, :, :, None]
    live_mask = jnp.broadcast_to(
        live_mask, (query_count, owner_count, slot_count, block_rows)
    ).reshape(query_count, -1)
    hard_max = jnp.max(jnp.where(live_mask, hard_logits, -jnp.inf), axis=1)
    group_rows = lax.all_gather(passages[0], "pb", axis=0, tiled=True)
    in_logits = (
        jnp.einsum("qd,kd->qk", query_rows, group_rows, preferred_element_type=jnp.float32)
        * score_scale
    )
    row_max = jnp.maximum(jnp.max(in_logits, axis=1), hard_max)
    row_total = jnp.sum(jnp.exp(in_logits - row_max[:, None]), axis=1)
    row_total = row_total + jnp.sum(
        jnp.where(live_mask, jnp.exp(hard_logits - row_max[:, None]), 0.0), axis=1
    )
    row_lse = row_max + jnp.log(row_total)
    picked = jnp.take_along_axis(in_logits, labels[:, None], axis=1)[:, 0]
    losses = row_lse - picked
    column_ids = jnp.arange(in_logits.shape[1], dtype=jnp.int32)
    target = (column_ids[None, :] == labels[:, None]).astype(jnp.float32)
    in_weights = ((jnp.exp(in_logits - row_lse[:, None]) - target) * score_scale).astype(
        jnp.bfloat16
    )
    passage_grads = lax.psum_scatter(
        jnp.einsum("qk,qd->kd", in_weights, query_rows, preferred_element_type=jnp.float32),
        "pb",
        scatter_dimension=0,
        tiled=True,
    )
    hard_weights = (
        jnp.where(live_mask, jnp.exp(hard_logits - row_lse[:, None]), 0.0) * score_scale
    ).astype(jnp.bfloat16)
    block_terms = jnp.einsum(
        "qr,qd->rd", hard_weights, query_rows, preferred_element_type=jnp.float32
    )
    block_terms = block_terms.reshape(owner_count, slot_count, block_rows, feature_width)
    returned_terms = lax.all_to_all(block_terms, "enc", split_axis=0, concat_axis=0, tiled=True)
    asked_ids = asked.reshape(-1)
    one_hot = (jnp.arange(local_blocks, dtype=jnp.int32)[:, None] == asked_ids[None, :]).astype(
        jnp.float32
    )
    table_grads = jnp.einsum(
        "bs,sx->bx",
        one_hot,
        returned_terms.reshape(asked_ids.shape[0], -1),
        precision=lax.Precision.HIGHEST,
    )
    table_grads = table_grads.reshape(1, local_blocks, block_rows, feature_width)
    return (losses[None], passage_grads[None], table_grads)


def solution(mesh):
    in_specs = (
        P("enc", "pb", None),
        P("enc", "pb", None),
        P("pb", "enc", None, None),
        P("enc", "pb", None),
        P("enc", "pb", None, None),
        P("enc", "pb", None),
        P("enc", "pb"),
    )
    out_specs = (P("enc", "pb"), P("enc", "pb", None), P("pb", "enc", None, None))
    return jax.shard_map(body, mesh=mesh, in_specs=in_specs, out_specs=out_specs, check_vma=False)
```

profile of v0, /device:TPU:6, one launch (start us, length us, event | category | flops | bytes accessed | tf_op | source)
XLA Modules:
  0.0 208.6 jit_solution(5770253707850789776)
XLA Ops:
  7.2 0.0 copy-start
  7.2 1.5 copy.42
  8.7 17.2 %all-to-all-start = ((s32[64,1,1]{2,1,0:T(1,128)}), s32[64,1,1]{2,1,0:T(1,128)S(1)}, u32[]{:S(2)}, u32[]{:S(2)}) async-start(s32[64,1,1]{2,1,0:T(1,128)} %copy.42), calls=%async_computation | async-start | bytes 65536 | tf_op jit(solution)/shard_map/all_to_all | solution.py:18
  25.8 0.0 all-gather.3.cloned.1.call-start
  25.9 0.7 all-gather.3.cloned.1.call-update
  26.6 7.1 %all-to-all-done = s32[64,1,1]{2,1,0:T(1,128)S(1)} async-done(((s32[64,1,1]{2,1,0:T(1,128)}), s32[64,1,1]{2,1,0:T(1,128)S(1)}, u32[]{:S(2)}, u32[]{:S(2)}) %all-to-all-start) | async-done | bytes 288 | tf_op jit(solution)/shard_map/all_to_all | solution.py:18
  33.7 1.2 reduce
  35.0 3.7 %gather_fusion = bf16[64,2,4096]{2,1,0:T(2,128)(2,1)S(1)} fusion(bf16[32,2,4096]{2,1,0:T(2,128)(2,1)} %bitcast.89, s32[1024]{0:T(1024)S(1)} %pad_clamp_fusion), kind=kCustom, calls=%fused_computation | custom fusion | bytes 2097408 | tf_op jit(solution)/shard_map/jit(_take)/gather | solution.py:19
  38.7 0.0 copy-start.1
  38.7 0.0 copy-start.3
  38.7 2.0 broadcast_select_fusion
  40.7 7.1 %all-to-all-start.1 = ((bf16[64,1,2,4096]{3,2,1,0:T(2,128)(2,1)}), bf16[64,1,2,4096]{3,2,1,0:T(2,128)(2,1)}, u32[]{:S(2)}, u32[]{:S(2)}) async-start(bf16[64,1,2,4096]{3,2,1,0:T(2,128)(2,1)} %broadcast_select_fusion), calls=%async_computation.1 | async-start | bytes 2097152 | tf_op jit(solution)/shard_map/all_to_all | solution.py:21
  47.8 0.0 copy-done.1
  47.9 0.1 fusion.19
  48.0 0.0 copy-done.3
  48.0 0.1 broadcast_and_fusion
  48.1 0.1 broadcast_in_dim.41
  48.2 0.1 reshape.321
  48.3 0.1 copy.43
  48.4 56.6 %all-gather.3.cloned.1.call-done = bf16[1,128,4096]{2,1,0:T(8,128)(2,1)} async-done(((bf16[1,8,4096]{2,1,0:T(8,128)(2,1)}), bf16[1,128,4096]{2,1,0:T(8,128)(2,1)}) %all-gather.3.cloned.1.call-update) | async-done | bytes 1048592 | tf_op jit(solution)/shard_map/all_gather | solution.py:37
  105.0 0.0 copy-done
  105.0 1.9 fusion.37
  106.9 0.0 all-to-all-done.1
  106.9 1.5 reshape.322
  108.3 0.7 select_reduce_fusion.1
  109.0 0.2 select_reduce_fusion
  109.3 0.1 fusion.21
  109.4 0.1 copy.46
  109.6 0.4 convolution_bitcast_fusion
  110.0 2.9 %copy.48 = f32[64,1,2,4096]{3,2,1,0:T(2,128)} copy(f32[64,1,2,4096]{3,0,2,1:T(8,128)S(1)} %convolution_bitcast_fusion) | data formatting | bytes 4194304 | tf_op jit(solution)/shard_map/qr,qd->rd/dot_general | solution.py:64
  112.9 0.0 copy-start.2
  112.9 10.6 %all-to-all-start.2 = ((f32[64,1,2,4096]{3,2,1,0:T(2,128)}), f32[64,1,2,4096]{3,2,1,0:T(2,128)}, u32[]{:S(2)}, u32[]{:S(2)}) async-start(f32[64,1,2,4096]{3,2,1,0:T(2,128)} %copy.48), calls=%async_computation.3 | async-start | bytes 4194304 | tf_op jit(solution)/shard_map/all_to_all | solution.py:68
  123.5 0.2 reduce-scatter.2.cloned.1.call-start
  123.7 0.0 copy-done.2
  123.8 1.9 fusion.3
  125.6 0.0 reduce-scatter.2.cloned.1.call-update
  125.7 1.6 gather_fusion.1
  127.3 0.6 fusion.31
  127.8 46.9 %all-to-all-done.2 = f32[64,1,2,4096]{3,2,1,0:T(2,128)} async-done(((f32[64,1,2,4096]{3,2,1,0:T(2,128)}), f32[64,1,2,4096]{3,2,1,0:T(2,128)}, u32[]{:S(2)}, u32[]{:S(2)}) %all-to-all-start.2) | async-done | bytes 2097184 | tf_op jit(solution)/shard_map/all_to_all | solution.py:68
  174.7 3.6 %convolution_bitcast_fusion.1 = f32[1,32,2,4096]{3,1,2,0:T(8,128)S(1)} fusion(s32[64]{0:T(128)S(1)} %reduce, f32[8,8,2,4096]{3,2,1,0:T(2,128)} %bitcast.29), kind=kOutput, calls=%fused_computation.3 | convolution fusion | flops 201328640 | bytes 3145984 | tf_op jit(solution)/shard_map/bs,sx->bx/dot_general | solution.py:73
  178.3 1.8 copy.50
  180.1 21.7 %reduce-scatter.2.cloned.1.call-done = f32[8,4096]{1,0:T(8,128)} async-done(((f32[128,4096]{1,0:T(8,128)}), f32[8,4096]{1,0:T(8,128)}) %reduce-scatter.2.cloned.1.call-update) | async-done | bytes 131088 | tf_op jit(solution)/shard_map/reduce_scatter | solution.py:55
  (12 shorter events, 0.1 us)
Async XLA Ops:
  7.2 97.8 %copy-start = (bf16[1,192,4096]{2,1,0:T(8,128)(2,1)S(1)}, bf16[1,192,4096]{2,1,0:T(8,128)(2,1)}, u32[]{:S(2)}) copy-start(bf16[1,192,4096]{2,1,0:T(8,128)(2,1)} %param.7) | copy-start | bytes 4718596
  8.7 25.1 %all-to-all-start = ((s32[64,1,1]{2,1,0:T(1,128)}), s32[64,1,1]{2,1,0:T(1,128)S(1)}, u32[]{:S(2)}, u32[]{:S(2)}) async-start(s32[64,1,1]{2,1,0:T(1,128)} %copy.42), calls=%async_computation | async-start | bytes 65536 | tf_op jit(solution)/shard_map/all_to_all | solution.py:18
  25.8 79.1 %all-gather.3.cloned.1.call-start = ((), (), s32[]{:S(2)}) async-start(), calls=%async_computation.5 | async-start | bytes 1114112 | tf_op jit(solution)/shard_map/all_gather | solution.py:37
  38.7 9.2 %copy-start.1 = (s32[1,192,16]{1,2,0:T(8,128)S(1)}, s32[1,192,16]{1,2,0:T(8,128)}, u32[]{:S(2)}) copy-start(s32[1,192,16]{1,2,0:T(8,128)} %param.10) | copy-start | bytes 36868
  38.7 9.3 %copy-start.3 = (s32[1,1,64]{2,1,0:T(1,128)S(1)}, s32[1,1,64]{2,1,0:T(1,128)}, u32[]{:S(2)}) copy-start(s32[1,1,64]{2,1,0:T(1,128)} %param.12) | copy-start | bytes 772
  40.7 66.1 %all-to-all-start.1 = ((bf16[64,1,2,4096]{3,2,1,0:T(2,128)(2,1)}), bf16[64,1,2,4096]{3,2,1,0:T(2,128)(2,1)}, u32[]{:S(2)}, u32[]{:S(2)}) async-start(bf16[64,1,2,4096]{3,2,1,0:T(2,128)(2,1)} %broadcast_select_fusion), calls=%async_computation.1 | async-start | bytes 2097152 | tf_op jit(solution)/shard_map/all_to_all | solution.py:21
  112.9 10.8 %copy-start.2 = (s32[1,192]{1,0:T(1,128)S(1)}, s32[1,192]{1,0:T(1,128)}, u32[]{:S(2)}) copy-start(s32[1,192]{1,0:T(1,128)} %param.13) | copy-start | bytes 2308
  112.9 61.8 %all-to-all-start.2 = ((f32[64,1,2,4096]{3,2,1,0:T(2,128)}), f32[64,1,2,4096]{3,2,1,0:T(2,128)}, u32[]{:S(2)}, u32[]{:S(2)}) async-start(f32[64,1,2,4096]{3,2,1,0:T(2,128)} %copy.48), calls=%async_computation.3 | async-start | bytes 4194304 | tf_op jit(solution)/shard_map/all_to_all | solution.py:68
  123.5 78.3 %reduce-scatter.2.cloned.1.call-start = ((), (), s32[]{:S(2)}) async-start(), calls=%async_computation.4 | async-start | bytes 2228224 | tf_op jit(solution)/shard_map/reduce_scatter | solution.py:55
Sparse Core Ops, SparseCore 0:
  29.3 75.5 all-gather.2
  128.3 73.4 reduce-scatter.1
where the time goes:
time: 210 us; the launch traced here: 209 us
  waiting for transfers between devices  133 us (63%)
  starting transfers between devices  35.1 us (17%)
  between operations  14.3 us (7%)
  local copies, waits for them, and re-layouts  13.4 us (6%)
  matrix products  8.39 us (4%)
  other arithmetic  4.46 us (2%)
    all_gather x1, waiting for transfers between devices, body(): group_rows = lax.all_gather(passages[0], 'pb', axis=0, tiled=True)  56.6 us
    all_to_all x1, waiting for transfers between devices, body(): lax.all_to_all(block_terms, 'enc', split_axis=0, concat_axis=0, tiled=True)  46.9 us
    reduce_scatter x1, waiting for transfers between devices, body(): lax.psum_scatter(jnp.einsum('qk,qd->kd', in_weights, query_rows, preferre...  21.7 us
    all_to_all x1, starting transfers between devices, body(): lax.all_to_all(block_lists[0, 0], 'enc', split_axis=0, concat_axis=0, til...  17.2 us
    all_to_all x1, starting transfers between devices, body(): lax.all_to_all(block_terms, 'enc', split_axis=0, concat_axis=0, tiled=True)  10.6 us
    all_to_all x1, waiting for transfers between devices, body(): lax.all_to_all(block_lists[0, 0], 'enc', split_axis=0, concat_axis=0, til...  7.13 us
    all_to_all x1, starting transfers between devices, body(): lax.all_to_all(chosen, 'enc', split_axis=0, concat_axis=0, tiled=True)  7.09 us
  transfers between devices with their start and end apart: 5, of which 4 were waited for; matrix products, arithmetic and copies ran while one was open for 9% of the time, Pallas kernels for 0%

commit v1 on v0

v1 whole, which is shorter than its diff:
```python
import functools

import jax
import jax.numpy as jnp
from jax import lax
from jax.experimental import pallas as pl
from jax.experimental.pallas import tpu as pltpu
from jax.sharding import PartitionSpec as P

score_scale = 50.0
lanes = 128
chips_x = 4
cores = 2
f32 = jnp.float32
bf16 = jnp.bfloat16


def partner(me, step, count):
    per_row = chips_x * cores
    rows = count // per_row
    y = lax.rem(me // per_row + step // per_row, rows)
    x = lax.rem((me // cores) % chips_x + (step // cores) % chips_x, chips_x)
    core = lax.rem(me % cores + step % cores, cores)
    return (y * chips_x + x) * cores + core


def exchange_kernel(
    n,
    m,
    q_hbm,
    p_ref,
    table_hbm,
    neg_ref,
    lists_ref,
    counts_ref,
    pos_ref,
    losses_ref,
    pgrad_ref,
    terms_ref,
    ids_ref,
    q_v,
    table_v,
    id_send,
    id_recv,
    id_scalars,
    fsend,
    fetched,
    wide,
    hard,
    pg,
    hard_w,
    in_w,
    pgp,
    tsend,
    rs_send,
    rs_recv,
    local_sem,
    id_sems,
    f_sems,
    t_sems,
    g_send,
    g_recv,
    r_send,
    r_recv,
):
    e = lax.axis_index("enc")
    z = lax.axis_index("pb")
    fwd = m // 2
    bwd = m - 1 - fwd
    up = lax.rem(z + 1, m)
    down = lax.rem(z + m - 1, m)
    pieces = fetched.shape[1]
    groups = pieces // 2
    width = q_v.shape[1]
    half = width // 2
    queries = q_v.shape[0]
    blocks = table_v.shape[0]

    barrier = pltpu.get_barrier_semaphore()

    def greet(s, carry):
        pl.semaphore_signal(barrier, inc=1, device_id={"enc": partner(e, s, n)})
        return carry

    lax.fori_loop(1, n, greet, 0)
    pl.semaphore_signal(barrier, inc=1, device_id={"pb": up})
    pl.semaphore_signal(barrier, inc=1, device_id={"pb": down})
    q_copy = pltpu.make_async_copy(q_hbm, q_v, local_sem.at[0])
    q_copy.start()
    table_copy = pltpu.make_async_copy(table_hbm, table_v, local_sem.at[1])
    table_copy.start()

    owner_row = lax.broadcasted_iota(jnp.int32, (n, n), 0)
    owner_col = lax.broadcasted_iota(jnp.int32, (n, n), 1)
    own_ids = jnp.sum(
        jnp.where(owner_row == owner_col, jnp.broadcast_to(lists_ref[...], (n, n)), 0),
        axis=1,
        keepdims=True,
    )
    id_send[...] = jnp.broadcast_to(own_ids, (n, lanes)).reshape(n, 1, lanes)
    own_rows = p_ref[...].astype(f32)
    pg[z] = jnp.concatenate([own_rows[:, :half], own_rows[:, half:]], axis=0).astype(bf16)

    pl.semaphore_wait(barrier, n + 1)

    def pass_on(side, t):
        origin = lax.rem(z + m - t, m) if side == 0 else lax.rem(z + t, m)
        return pltpu.make_async_remote_copy(
            src_ref=pg.at[origin],
            dst_ref=pg.at[origin],
            send_sem=g_send.at[side, t],
            recv_sem=g_recv.at[side, t],
            device_id={"pb": up if side == 0 else down},
        )

    def arrival(side, t):
        origin = lax.rem(z + m - t - 1, m) if side == 0 else lax.rem(z + t + 1, m)
        return pltpu.make_async_remote_copy(
            src_ref=pg.at[origin],
            dst_ref=pg.at[origin],
            send_sem=g_send.at[side, t],
            recv_sem=g_recv.at[side, t],
            device_id={"pb": up if side == 0 else down},
        )

    def ask(s, carry):
        peer = partner(e, s, n)
        pltpu.make_async_remote_copy(
            src_ref=id_send.at[peer],
            dst_ref=id_recv.at[e],
            send_sem=id_sems.at[0],
            recv_sem=id_sems.at[1],
            device_id={"enc": peer},
        ).start()
        return carry

    lax.fori_loop(1, n, ask, 0)
    pltpu.make_async_copy(id_send.at[e], id_recv.at[e], id_sems.at[1]).start()
    pass_on(0, 0).start()
    pass_on(1, 0).start()
    table_copy.wait()
    pltpu.make_async_copy(id_recv, id_recv, id_sems.at[1]).wait()
    scalar_copy = pltpu.make_async_copy(id_recv, id_scalars, local_sem.at[2])
    scalar_copy.start()
    scalar_copy.wait()

    def serve(s, carry):
        peer = partner(e, s, n)
        wanted = id_scalars[peer, 0, 0]
        ids_ref[peer] = wanted
        fsend[peer] = table_v[wanted]
        pltpu.make_async_remote_copy(
            src_ref=fsend.at[peer],
            dst_ref=fetched.at[e],
            send_sem=f_sems.at[0],
            recv_sem=f_sems.at[1],
            device_id={"enc": peer},
        ).start()
        return carry

    lax.fori_loop(1, n, serve, 0)
    own_wanted = id_scalars[e, 0, 0]
    ids_ref[e] = own_wanted
    fetched[e] = table_v[own_wanted]

    for t in range(fwd):
        arrival(0, t).wait_recv()
        if t + 1 < fwd:
            pass_on(0, t + 1).start()
        if t < bwd:
            arrival(1, t).wait_recv()
        if t + 1 < bwd:
            pass_on(1, t + 1).start()

    q_copy.wait()
    contract_last = (((1,), (1,)), ((), ()))
    all_rows = pg[...].reshape(m * 16, half)
    first = lax.dot_general(all_rows, q_v[:, :half], contract_last, preferred_element_type=f32)
    second = lax.dot_general(all_rows, q_v[:, half:], contract_last, preferred_element_type=f32)
    first = first.reshape(m, 2, 8, queries)[:, 0]
    second = second.reshape(m, 2, 8, queries)[:, 1]
    in_logits = ((first + second) * score_scale).reshape(m * 8, queries)

    owner_ids = lax.div(neg_ref[...], blocks)
    owner_list = lax.broadcasted_iota(jnp.int32, (n, queries), 0)
    named = jnp.zeros((n, queries), jnp.bool_)
    for k in range(neg_ref.shape[0]):
        named = named | (owner_list == jnp.broadcast_to(owner_ids[k : k + 1, :], (n, queries)))
    usable = jnp.sum(
        jnp.where(owner_row == owner_col, jnp.broadcast_to(counts_ref[...], (n, n)), 0),
        axis=1,
        keepdims=True,
    )
    live = jnp.where(named, jnp.broadcast_to(usable, (n, queries)), 0)
    live = jnp.concatenate([live, live], axis=0) > 0

    pltpu.make_async_copy(
        fetched.at[pl.ds(0, n - 1)], fetched.at[pl.ds(0, n - 1)], f_sems.at[1]
    ).wait()

    def widen(o, carry):
        wide[pl.ds(pl.multiple_of(o * pieces, pieces), pieces), :] = fetched[o].astype(f32)
        return carry

    lax.fori_loop(0, n, widen, 0, unroll=4)
    for j in range(groups):
        both = [wide[pl.ds(2 * j + r, n, pieces), :] for r in range(2)]
        hard[:, j * lanes : (j + 1) * lanes] = jnp.concatenate(both, axis=0).astype(bf16)
    hard_logits = (
        lax.dot_general(hard[...], q_v[...], contract_last, preferred_element_type=f32)
        * score_scale
    )

    top = jnp.maximum(
        jnp.max(in_logits, axis=0, keepdims=True),
        jnp.max(jnp.where(live, hard_logits, -jnp.inf), axis=0, keepdims=True),
    )
    total = jnp.sum(jnp.exp(in_logits - top), axis=0, keepdims=True) + jnp.sum(
        jnp.where(live, jnp.exp(hard_logits - top), 0.0), axis=0, keepdims=True
    )
    row_lse = top + jnp.log(total)
    hard_weights = jnp.where(live, jnp.exp(hard_logits - row_lse), 0.0) * score_scale
    hard_w[...] = hard_weights.astype(bf16)
    is_label = lax.broadcasted_iota(jnp.int32, in_logits.shape, 0) == pos_ref[...]
    picked = jnp.sum(jnp.where(is_label, in_logits, 0.0), axis=0, keepdims=True)
    losses_ref[...] = row_lse - picked
    in_weights = (jnp.exp(in_logits - row_lse) - jnp.where(is_label, 1.0, 0.0)) * score_scale
    in_w[...] = in_weights.astype(bf16)

    span = 4 * lanes
    for c in range(width // span):
        part = jnp.dot(
            hard_w[...], q_v[:, c * span : (c + 1) * span], preferred_element_type=f32
        )
        for k in range(4):
            for r in range(2):
                wide[pl.ds(2 * (4 * c + k) + r, n, pieces), :] = part[
                    r * n : (r + 1) * n, k * lanes : (k + 1) * lanes
                ]

    def give(s, carry):
        peer = partner(e, s, n)
        tsend[peer] = wide[pl.ds(pl.multiple_of(peer * pieces, pieces), pieces), :].astype(bf16)
        pltpu.make_async_remote_copy(
            src_ref=tsend.at[peer],
            dst_ref=terms_ref.at[e],
            send_sem=t_sems.at[0],
            recv_sem=t_sems.at[1],
            device_id={"enc": peer},
        ).start()
        return carry

    lax.fori_loop(1, n, give, 0)
    tsend[e] = wide[pl.ds(pl.multiple_of(e * pieces, pieces), pieces), :].astype(bf16)
    pltpu.make_async_copy(tsend.at[e], terms_ref.at[e], t_sems.at[1]).start()

    for c in range(width // span):
        part = jnp.dot(
            in_w[...], q_v[:, c * span : (c + 1) * span], preferred_element_type=f32
        )
        h, at = divmod(c * span, half)
        pgp[:, 8 * h : 8 * h + 8, at : at + span] = part.reshape(m, 8, span)

    def carry_on(side, t):
        return pltpu.make_async_remote_copy(
            src_ref=rs_send.at[side, t],
            dst_ref=rs_recv.at[side, t],
            send_sem=r_send.at[side, t],
            recv_sem=r_recv.at[side, t],
            device_id={"pb": up if side == 0 else down},
        )

    for t in range(fwd):
        for side in range(2):
            steps = bwd if side else fwd
            if t >= steps:
                continue
            target = lax.rem(z + m - (steps - t), m) if side else lax.rem(z + steps - t, m)
            held = pgp[target]
            if t > 0:
                carry_on(side, t - 1).wait_recv()
                held = held + rs_recv[side, t - 1].astype(f32)
            rs_send[side, t] = held.astype(bf16)
            carry_on(side, t).start()
    carry_on(0, fwd - 1).wait_recv()
    carry_on(1, bwd - 1).wait_recv()
    done = pgp[z] + rs_recv[0, fwd - 1].astype(f32) + rs_recv[1, bwd - 1].astype(f32)
    pgrad_ref[:, :half] = done[:8]
    pgrad_ref[:, half:] = done[8:]

    pltpu.make_async_copy(
        id_send.at[pl.ds(0, n - 1)], id_send.at[pl.ds(0, n - 1)], id_sems.at[0]
    ).wait()
    pltpu.make_async_copy(
        fsend.at[pl.ds(0, n - 1)], fsend.at[pl.ds(0, n - 1)], f_sems.at[0]
    ).wait()
    for side in range(2):
        for t in range(bwd if side else fwd):
            pass_on(side, t).wait_send()
            carry_on(side, t).wait_send()
    pltpu.make_async_copy(
        tsend.at[pl.ds(0, n - 1)], tsend.at[pl.ds(0, n - 1)], t_sems.at[0]
    ).wait()
    pltpu.make_async_copy(terms_ref, terms_ref, t_sems.at[1]).wait()


def collect_kernel(ids_ref, terms_ref, out_ref):
    out_ref[...] = jnp.zeros_like(out_ref)

    def add(s, carry):
        block = ids_ref[s]
        out_ref[block] += terms_ref[s].astype(f32)
        return carry

    lax.fori_loop(0, terms_ref.shape[0], add, 0)


def body(queries, passages, table, neg_blocks, block_lists, block_counts, pos_index):
    n = lax.axis_size("enc")
    m = lax.axis_size("pb")
    query_rows = queries[0]
    count, width = query_rows.shape
    blocks = table.shape[1]
    pieces = 2 * width // lanes
    table_rows = (
        table[0]
        .reshape(blocks, 2, width // lanes, lanes)
        .transpose(0, 2, 1, 3)
        .reshape(blocks, pieces, lanes)
    )
    whole = pl.BlockSpec(memory_space=pltpu.VMEM)
    anywhere = pl.BlockSpec(memory_space=pl.ANY)
    losses, passage_grads, terms, ids = pl.pallas_call(
        functools.partial(exchange_kernel, n, m),
        out_shape=(
            jax.ShapeDtypeStruct((1, count), f32),
            jax.ShapeDtypeStruct((8, width), f32),
            jax.ShapeDtypeStruct((n, pieces, lanes), bf16),
            jax.ShapeDtypeStruct((n,), jnp.int32),
        ),
        in_specs=[anywhere, whole, anywhere, whole, whole, whole, whole],
        out_specs=(whole, whole, anywhere, pl.BlockSpec(memory_space=pltpu.SMEM)),
        scratch_shapes=[
            pltpu.VMEM((count, width), bf16),
            pltpu.VMEM((blocks, pieces, lanes), bf16),
            pltpu.VMEM((n, 1, lanes), jnp.int32),
            pltpu.VMEM((n, 1, lanes), jnp.int32),
            pltpu.SMEM((n, 1, lanes), jnp.int32),
            pltpu.VMEM((n, pieces, lanes), bf16),
            pltpu.VMEM((n, pieces, lanes), bf16),
            pltpu.VMEM((n * pieces, lanes), f32),
            pltpu.VMEM((2 * n, width), bf16),
            pltpu.VMEM((m, 16, width // 2), bf16),
            pltpu.VMEM((2 * n, count), bf16),
            pltpu.VMEM((8 * m, count), bf16),
            pltpu.VMEM((m, 16, width // 2), f32),
            pltpu.VMEM((n, pieces, lanes), bf16),
            pltpu.VMEM((2, m // 2, 16, width // 2), bf16),
            pltpu.VMEM((2, m // 2, 16, width // 2), bf16),
            pltpu.SemaphoreType.DMA((3,)),
            pltpu.SemaphoreType.DMA((2,)),
            pltpu.SemaphoreType.DMA((2,)),
            pltpu.SemaphoreType.DMA((2,)),
            pltpu.SemaphoreType.DMA((2, m // 2)),
            pltpu.SemaphoreType.DMA((2, m // 2)),
            pltpu.SemaphoreType.DMA((2, m // 2)),
            pltpu.SemaphoreType.DMA((2, m // 2)),
        ],
        compiler_params=pltpu.CompilerParams(
            collective_id=0, has_side_effects=True, vmem_limit_bytes=40 << 20
        ),
        name="exchange",
    )(
        query_rows,
        passages[0],
        table_rows,
        neg_blocks[0].T,
        block_lists[0, 0].reshape(1, n),
        block_counts[0],
        pos_index,
    )
    table_grads = pl.pallas_call(
        collect_kernel,
        out_shape=jax.ShapeDtypeStruct((blocks, pieces, lanes), f32),
        in_specs=[pl.BlockSpec(memory_space=pltpu.SMEM), whole],
        out_specs=whole,
        compiler_params=pltpu.CompilerParams(vmem_limit_bytes=16 << 20),
        name="collect",
    )(ids, terms)
    table_grads = (
        table_grads.reshape(blocks, width // lanes, 2, lanes)
        .transpose(0, 2, 1, 3)
        .reshape(1, blocks, 2, width)
    )
    return (losses, passage_grads[None], table_grads)


def solution(mesh):
    in_specs = (
        P("enc", "pb", None),
        P("enc", "pb", None),
        P("pb", "enc", None, None),
        P("enc", "pb", None),
        P("enc", "pb", None, None),
        P("enc", "pb", None),
        P("enc", "pb"),
    )
    out_specs = (P("enc", "pb"), P("enc", "pb", None), P("pb", "enc", None, None))
    return jax.shard_map(body, mesh=mesh, in_specs=in_specs, out_specs=out_specs, check_vma=False)
```

time: 210 us -> 102 us (0.49)
  waiting for transfers between devices: 133 us -> 0 us
  Pallas kernels: 0 us -> 93.8 us
  starting transfers between devices: 35.1 us -> 0 us
  between operations: 14.3 us -> 0.66 us
  matrix products: 8.39 us -> 0 us
  local copies, waits for them, and re-layouts: 13.4 us -> 7.2 us
  other arithmetic: 4.46 us -> 0 us
    pallas_call x0 -> x2, Pallas kernels: none -> 93.8 us  [the longest x1 91.7 us: body(): pl.pallas_call(functools.partial(exchange_kernel, n, m), out_shape=(jax.S...]
    all_gather x1 -> x0, waiting for transfers between devices: 56.6 us -> none  [body(): group_rows = lax.all_gather(passages[0], 'pb', axis=0, tiled=True)]
    all_to_all x3 -> x0, waiting for transfers between devices: 54 us -> none  [the longest x1 46.9 us: body(): lax.all_to_all(block_terms, 'enc', split_axis=0, concat_axis=0, tiled=True)]
    all_to_all x3 -> x0, starting transfers between devices: 34.8 us -> none  [the longest x1 17.2 us: body(): lax.all_to_all(block_lists[0, 0], 'enc', split_axis=0, concat_axis=0, til...]
    reduce_scatter x1 -> x0, waiting for transfers between devices: 21.7 us -> none  [body(): lax.psum_scatter(jnp.einsum('qk,qd->kd', in_weights, query_rows, preferre...]
    dot_general x5 -> x0, matrix products: 8.39 us -> none  [the longest x1 3.56 us: body(): jnp.einsum('bs,sx->bx', one_hot, returned_terms.reshape(asked_ids.shape[0...]
    unnamed x10 -> x16, local copies, waits for them, and re-layouts: 1.81 us -> 7.2 us
    gather x2 -> x0, local copies, waits for them, and re-layouts: 5.27 us -> none  [the longest x1 3.7 us: body(): chosen = jnp.take(table[0], asked.reshape(-1), axis=0)]
  transfers between devices with their start and end apart: 5 -> 0, of which waited for: 4 -> 0; matrix products, arithmetic and copies ran while one was open for 9% -> 0% of each run, Pallas kernels for 0% -> 0%
where the time goes in v1:
time: 102 us
  Pallas kernels  93.8 us (92%)
  local copies, waits for them, and re-layouts  7.2 us (7%)
    pallas_call x1, Pallas kernels, body(): pl.pallas_call(functools.partial(exchange_kernel, n, m), out_shape=(jax.S...  91.7 us
    unnamed x16, local copies, waits for them, and re-layouts  7.2 us
    pallas_call x1, Pallas kernels, body(): pl.pallas_call(collect_kernel, out_shape=jax.ShapeDtypeStruct((blocks, pi...  2.08 us

profile of v1, /device:TPU:6, one launch (start us, length us, event | category | flops | bytes accessed | tf_op | source)
XLA Modules:
  0.0 101.7 jit_solution(11746150286415851143)
XLA Ops:
  0.6 0.0 copy-start
  0.6 1.4 %copy-done = bf16[1,192,4096]{2,1,0:T(8,128)(2,1)S(1)} copy-done((bf16[1,192,4096]{2,1,0:T(8,128)(2,1)S(1)}, bf16[1,192,4096]{2,1,0:T(8,128)(2,1)}, u32[]{:S(2)}) %copy-start) | copy-done | bytes 1572888
  2.0 0.0 copy-start.1
  2.0 1.0 %copy-done.1 = bf16[1,32,2,4096]{3,2,1,0:T(2,128)(2,1)S(1)} copy-done((bf16[1,32,2,4096]{3,2,1,0:T(2,128)(2,1)S(1)}, bf16[1,32,2,4096]{3,2,1,0:T(2,128)(2,1)}, u32[]{:S(2)}) %copy-start.1) | copy-done | bytes 524312
  3.1 0.0 copy-start.2
  3.1 0.8 copy-done.2
  3.9 0.0 copy-start.3
  3.9 0.7 copy-done.3
  4.6 0.0 copy-start.4
  4.6 0.7 copy-done.4
  5.3 0.0 copy-start.5
  5.3 0.7 copy-done.5
  6.0 0.0 copy-start.6
  6.0 0.7 copy-done.6
  6.6 91.7 %exchange.1 = (f32[1,192]{1,0:T(1,128)S(1)}, f32[8,4096]{1,0:T(8,128)S(1)}, bf16[64,64,128]{2,1,0:T(8,128)(2,1)S(1)}, s32[64]{0:T(128)S(1)}) custom-call(bf16[192,4096]{1,0:T(8,128)(2,1)S(1)} %bitcast.18, bf16[8,4096]{1,0:T(8,128)(2,1)S(1)} %bitcast.21, bf16[32,64,128]{2,1,0:T(8,128)(2,1)S(1)} %bitcast.19, s32[16,192]{1,0:T(8,128)S(1)} %bitcast.22, ...), custom_call_target="tpu_custom_call" | custom-call | tf_op jit(solution)/shard_map/exchange/pallas_call | solution.py:333
  98.4 2.1 %collect.1 = f32[32,64,128]{2,1,0:T(8,128)} custom-call(s32[64]{0:T(128)S(1)} %get-tuple-element.9.ids_ref, bf16[64,64,128]{2,1,0:T(8,128)(2,1)S(1)} %get-tuple-element.10.terms_ref), custom_call_target="tpu_custom_call" | custom-call | tf_op jit(solution)/shard_map/collect/pallas_call | solution.py:382
  100.5 0.6 copy.14
  101.0 0.7 copy.15
Async XLA Ops:
  0.6 1.4 %copy-start = (bf16[1,192,4096]{2,1,0:T(8,128)(2,1)S(1)}, bf16[1,192,4096]{2,1,0:T(8,128)(2,1)}, u32[]{:S(2)}) copy-start(bf16[1,192,4096]{2,1,0:T(8,128)(2,1)} %param.7) | copy-start | bytes 4718596
  2.0 1.0 %copy-start.1 = (bf16[1,32,2,4096]{3,2,1,0:T(2,128)(2,1)S(1)}, bf16[1,32,2,4096]{3,2,1,0:T(2,128)(2,1)}, u32[]{:S(2)}) copy-start(bf16[1,32,2,4096]{3,2,1,0:T(2,128)(2,1)} %param.9) | copy-start | bytes 1572868
  3.1 0.8 copy-start.2
  3.9 0.7 copy-start.3
  4.6 0.7 copy-start.4
  5.3 0.7 copy-start.5
  6.0 0.7 copy-start.6

commit v2 on v1

v2 whole, which is shorter than its diff:
```python
import functools

import jax
import jax.numpy as jnp
from jax import lax
from jax.experimental import pallas as pl
from jax.experimental.pallas import tpu as pltpu
from jax.sharding import PartitionSpec as P

score_scale = 50.0
lanes = 128
chips_x = 4
cores = 2
ring_cuts = 2
send_group = 16
collect_groups = 4
f32 = jnp.float32
bf16 = jnp.bfloat16


def zigzag(k, count):
    odd = k % 2
    return lax.rem(odd * ((k + 1) // 2) + (1 - odd) * (count - k // 2), count)


def partner(me, step, count):
    rows = count // (chips_x * cores)
    y = lax.rem(me // (chips_x * cores) + zigzag(step % rows, rows), rows)
    x = lax.rem((me // cores) % chips_x + zigzag((step // rows) % chips_x, chips_x), chips_x)
    core = lax.rem(me % cores + step // (rows * chips_x), cores)
    return (y * chips_x + x) * cores + core


def source(me, step, count):
    rows = count // (chips_x * cores)
    y = lax.rem(me // (chips_x * cores) + rows - zigzag(step % rows, rows), rows)
    x = lax.rem(
        (me // cores) % chips_x + chips_x - zigzag((step // rows) % chips_x, chips_x), chips_x
    )
    core = lax.rem(me % cores + step // (rows * chips_x), cores)
    return (y * chips_x + x) * cores + core


def exchange_kernel(
    n,
    m,
    q_hbm,
    p_hbm,
    table_hbm,
    neg_hbm,
    lists_hbm,
    counts_hbm,
    pos_hbm,
    losses_ref,
    pgrad_ref,
    terms_ref,
    ids_ref,
    q_v,
    p_ref,
    table_v,
    neg_ref,
    counts_ref,
    pos_ref,
    column_lists,
    all_lists,
    id_row,
    id_scalars,
    fsend,
    fetched,
    wide,
    hard,
    pg,
    hard_w,
    in_w,
    pgp,
    tsend,
    rs_send,
    rs_recv,
    local_sem,
    id_sems,
    f_sems,
    t_sems,
    g_send,
    g_recv,
    r_send,
    r_recv,
):
    e = lax.axis_index("enc")
    z = lax.axis_index("pb")
    fwd = m // 2
    bwd = m - 1 - fwd
    up = lax.rem(z + 1, m)
    down = lax.rem(z + m - 1, m)
    pieces = fetched.shape[1]
    groups = pieces // 2
    width = q_v.shape[1]
    cut_width = pg.shape[3]
    per_row = chips_x * cores
    rows = n // per_row
    row, place = e // per_row, e % per_row
    queries = q_v.shape[0]
    blocks = table_v.shape[0]

    barrier = pltpu.get_barrier_semaphore()

    def row_mate(k):
        return {"enc": row * per_row + lax.rem(place + k, per_row)}

    def column_mate(k):
        return {"enc": lax.rem(row + k, rows) * per_row + place}

    for k in range(1, per_row):
        pl.semaphore_signal(barrier, inc=1, device_id=row_mate(k))
    for k in range(1, rows):
        pl.semaphore_signal(barrier, inc=1, device_id=column_mate(k))
    pl.semaphore_signal(barrier, inc=1, device_id={"pb": up})
    pl.semaphore_signal(barrier, inc=1, device_id={"pb": down})
    loads = [
        pltpu.make_async_copy(source, place, local_sem.at[k])
        for k, (source, place) in enumerate(
            (
                (lists_hbm, column_lists.at[row]),
                (p_hbm, p_ref),
                (table_hbm, table_v),
                (counts_hbm, counts_ref),
                (neg_hbm, neg_ref),
                (pos_hbm, pos_ref),
                (q_hbm, q_v),
            )
        )
    ]
    for load in loads:
        load.start()

    owner_row = lax.broadcasted_iota(jnp.int32, (n, n), 0)
    owner_col = lax.broadcasted_iota(jnp.int32, (n, n), 1)
    loads[1].wait()
    own_rows = p_ref[...].astype(f32)
    for u in range(ring_cuts):
        at = 2 * u * cut_width
        halves = [own_rows[:, at + h * cut_width : at + (h + 1) * cut_width] for h in range(2)]
        pg[u, z] = jnp.concatenate(halves, axis=0).astype(bf16)
    loads[0].wait()

    pl.semaphore_wait(barrier, per_row + rows)

    def ring_copy(side, u, t, origin):
        return pltpu.make_async_remote_copy(
            src_ref=pg.at[u, origin],
            dst_ref=pg.at[u, origin],
            send_sem=g_send.at[side, u, t],
            recv_sem=g_recv.at[side, u, t],
            device_id={"pb": down if side else up},
        )

    def pass_on(side, u, t):
        return ring_copy(side, u, t, lax.rem(z + t if side else z + m - t, m))

    def arrival(side, u, t):
        return ring_copy(side, u, t, lax.rem(z + t + 1 if side else z + m - t - 1, m))

    def gather_step(t):
        for u in range(ring_cuts):
            for side, steps in ((0, fwd), (1, bwd)):
                if t < steps:
                    arrival(side, u, t).wait_recv()
                if t + 1 < steps:
                    pass_on(side, u, t + 1).start()

    def column_copy(k):
        return pltpu.make_async_remote_copy(
            src_ref=column_lists.at[row],
            dst_ref=column_lists.at[row],
            send_sem=id_sems.at[0],
            recv_sem=id_sems.at[1],
            device_id=column_mate(k),
        )

    def row_copy(k):
        return pltpu.make_async_remote_copy(
            src_ref=column_lists,
            dst_ref=all_lists.at[place],
            send_sem=id_sems.at[2],
            recv_sem=id_sems.at[3],
            device_id=row_mate(k),
        )

    def to_scalars(lists, slot):
        wanted = jnp.sum(
            jnp.where(owner_col[: lists.shape[0]] == e, lists, 0), axis=1, keepdims=True
        )
        id_row[slot] = jnp.sum(
            jnp.where(
                owner_row[: lists.shape[0]] == owner_col[: lists.shape[0]],
                jnp.broadcast_to(wanted, lists.shape),
                0,
            ),
            axis=0,
            keepdims=True,
        )
        copy = pltpu.make_async_copy(id_row.at[slot], id_scalars.at[slot], local_sem.at[7 + slot])
        copy.start()
        return copy

    def serve(slot, group, s, carry):
        peer = partner(e, s, n)
        asker = peer // per_row if slot == 0 else (peer % per_row) * rows + peer // per_row
        wanted = id_scalars[slot, 0, asker]
        ids_ref[peer] = wanted
        fsend[peer] = table_v[wanted]
        pltpu.make_async_remote_copy(
            src_ref=fsend.at[peer],
            dst_ref=fetched.at[e],
            send_sem=f_sems.at[0],
            recv_sem=f_sems.at[1 + group],
            device_id={"enc": peer},
        ).start()
        return carry

    for k in range(1, rows):
        column_copy(k).start()
    for u in range(ring_cuts):
        pass_on(0, u, 0).start()
        pass_on(1, u, 0).start()
    column_part = column_lists.at[pl.ds(0, rows - 1)]
    pltpu.make_async_copy(column_part, column_part, id_sems.at[1]).wait()
    for k in range(1, per_row):
        row_copy(k).start()
    early = to_scalars(column_lists[...].reshape(rows, n), 0)
    all_lists[place] = column_lists[...]
    loads[2].wait()
    early.wait()
    lax.fori_loop(1, rows, functools.partial(serve, 0, 0), 0)
    own_wanted = id_scalars[0, 0, row]
    ids_ref[e] = own_wanted
    fetched[e] = table_v[own_wanted]
    row_part = all_lists.at[pl.ds(0, per_row - 1)]
    pltpu.make_async_copy(row_part, row_part, id_sems.at[3]).wait()
    to_scalars(all_lists[...].reshape(n, n), 1).wait()

    quarter = n // 4
    for t in range(max(fwd, 4)):
        if t < 4:
            first = max(rows, t * quarter)
            lax.fori_loop(first, (t + 1) * quarter, functools.partial(serve, 1, t), 0)
        if t < fwd:
            gather_step(t)

    for load in loads[3:]:
        load.wait()
    contract_last = (((1,), (1,)), ((), ()))
    in_logits = jnp.zeros((m, 8, queries), f32)
    for u in range(ring_cuts):
        all_rows = pg[u].reshape(m * 16, cut_width)
        for h in range(2):
            at = (2 * u + h) * cut_width
            part = lax.dot_general(
                all_rows, q_v[:, at : at + cut_width], contract_last, preferred_element_type=f32
            )
            in_logits = in_logits + part.reshape(m, 2, 8, queries)[:, h]
    in_logits = in_logits.reshape(m * 8, queries) * score_scale

    owner_ids = lax.div(neg_ref[...], blocks)
    owner_list = lax.broadcasted_iota(jnp.int32, (n, queries), 0)
    named = jnp.zeros((n, queries), jnp.bool_)
    for k in range(neg_ref.shape[0]):
        named = named | (owner_list == jnp.broadcast_to(owner_ids[k : k + 1, :], (n, queries)))
    usable = jnp.sum(
        jnp.where(owner_row == owner_col, jnp.broadcast_to(counts_ref[...], (n, n)), 0),
        axis=1,
        keepdims=True,
    )
    live = jnp.where(named, jnp.broadcast_to(usable, (n, queries)), 0)
    live = jnp.concatenate([live, live], axis=0) > 0

    def widen(s, carry):
        origin = source(e, s, n)
        at = pl.ds(pl.multiple_of(origin * pieces, pieces), pieces)
        wide[at, :] = fetched[origin].astype(f32)
        return carry

    for t in range(4):
        count = quarter - 1 if t == 0 else quarter
        arrived = fetched.at[pl.ds(0, count)]
        pltpu.make_async_copy(arrived, arrived, f_sems.at[1 + t]).wait()
        lax.fori_loop(t * quarter, (t + 1) * quarter, widen, 0, unroll=4)
    for j in range(groups):
        both = [wide[pl.ds(2 * j + r, n, pieces), :] for r in range(2)]
        hard[:, j * lanes : (j + 1) * lanes] = jnp.concatenate(both, axis=0).astype(bf16)
    hard_logits = (
        lax.dot_general(hard[...], q_v[...], contract_last, preferred_element_type=f32)
        * score_scale
    )

    top = jnp.maximum(
        jnp.max(in_logits, axis=0, keepdims=True),
        jnp.max(jnp.where(live, hard_logits, -jnp.inf), axis=0, keepdims=True),
    )
    total = jnp.sum(jnp.exp(in_logits - top), axis=0, keepdims=True) + jnp.sum(
        jnp.where(live, jnp.exp(hard_logits - top), 0.0), axis=0, keepdims=True
    )
    row_lse = top + jnp.log(total)
    hard_weights = jnp.where(live, jnp.exp(hard_logits - row_lse), 0.0) * score_scale
    hard_w[...] = hard_weights.astype(bf16)
    is_label = lax.broadcasted_iota(jnp.int32, in_logits.shape, 0) == pos_ref[...]
    picked = jnp.sum(jnp.where(is_label, in_logits, 0.0), axis=0, keepdims=True)
    losses_ref[...] = row_lse - picked
    in_weights = (jnp.exp(in_logits - row_lse) - jnp.where(is_label, 1.0, 0.0)) * score_scale
    in_w[...] = in_weights.astype(bf16)

    span = 4 * lanes
    for c in range(width // span):
        part = jnp.dot(
            hard_w[...], q_v[:, c * span : (c + 1) * span], preferred_element_type=f32
        )
        for k in range(4):
            for r in range(2):
                wide[pl.ds(2 * (4 * c + k) + r, n, pieces), :] = part[
                    r * n : (r + 1) * n, k * lanes : (k + 1) * lanes
                ]

    def give(s, carry):
        peer = partner(e, s, n)
        tsend[peer] = wide[pl.ds(pl.multiple_of(peer * pieces, pieces), pieces), :].astype(bf16)
        pltpu.make_async_remote_copy(
            src_ref=tsend.at[peer],
            dst_ref=terms_ref.at[e],
            send_sem=t_sems.at[0],
            recv_sem=t_sems.at[1],
            device_id={"enc": peer},
        ).start()
        return carry

    lax.fori_loop(1, send_group, give, 0)
    tsend[e] = wide[pl.ds(pl.multiple_of(e * pieces, pieces), pieces), :].astype(bf16)
    pltpu.make_async_copy(tsend.at[e], terms_ref.at[e], t_sems.at[1]).start()

    for c in range(width // span):
        part = jnp.dot(
            in_w[...], q_v[:, c * span : (c + 1) * span], preferred_element_type=f32
        )
        u, at = divmod(c * span, 2 * cut_width)
        h, at = divmod(at, cut_width)
        pgp[u, :, 8 * h : 8 * h + 8, at : at + span] = part.reshape(m, 8, span)

    def carry_on(side, u, t):
        return pltpu.make_async_remote_copy(
            src_ref=rs_send.at[side, u, t],
            dst_ref=rs_recv.at[side, u, t],
            send_sem=r_send.at[side, u, t],
            recv_sem=r_recv.at[side, u, t],
            device_id={"pb": down if side else up},
        )

    def reduce_step(t):
        for u in range(ring_cuts):
            for side, steps in ((0, fwd), (1, bwd)):
                if t >= steps:
                    continue
                target = lax.rem(z + m - (steps - t) if side else z + steps - t, m)
                held = pgp[u, target]
                if t > 0:
                    carry_on(side, u, t - 1).wait_recv()
                    held = held + rs_recv[side, u, t - 1].astype(f32)
                rs_send[side, u, t] = held.astype(bf16)
                carry_on(side, u, t).start()

    for t in range(max(fwd, n // send_group)):
        if t < fwd:
            reduce_step(t)
        if t > 0 and t * send_group < n:
            lax.fori_loop(t * send_group, min(n, (t + 1) * send_group), give, 0)
    for u in range(ring_cuts):
        carry_on(0, u, fwd - 1).wait_recv()
        carry_on(1, u, bwd - 1).wait_recv()
        done = (
            pgp[u, z] + rs_recv[0, u, fwd - 1].astype(f32) + rs_recv[1, u, bwd - 1].astype(f32)
        )
        at = 2 * u * cut_width
        pgrad_ref[:, at : at + cut_width] = done[:8]
        pgrad_ref[:, at + cut_width : at + 2 * cut_width] = done[8:]

    pltpu.make_async_copy(column_part, column_part, id_sems.at[0]).wait()
    pltpu.make_async_copy(row_part, row_part, id_sems.at[2]).wait()
    pltpu.make_async_copy(
        fsend.at[pl.ds(0, n - 1)], fsend.at[pl.ds(0, n - 1)], f_sems.at[0]
    ).wait()
    for side in range(2):
        for t in range(bwd if side else fwd):
            for u in range(ring_cuts):
                pass_on(side, u, t).wait_send()
                carry_on(side, u, t).wait_send()
    pltpu.make_async_copy(
        tsend.at[pl.ds(0, n - 1)], tsend.at[pl.ds(0, n - 1)], t_sems.at[0]
    ).wait()
    pltpu.make_async_copy(terms_ref, terms_ref, t_sems.at[1]).wait()


def collect_kernel(
    ids_ref, terms_hbm, losses_ref, pgrad_ref, out_ref, losses_out, pgrad_out, terms_ref, sems
):
    copies = [
        pltpu.make_async_copy(losses_ref, losses_out, sems.at[0]),
        pltpu.make_async_copy(pgrad_ref, pgrad_out, sems.at[1]),
    ]
    group = terms_hbm.shape[0] // collect_groups
    for g in range(collect_groups):
        some = pl.ds(g * group, group)
        copies.append(
            pltpu.make_async_copy(terms_hbm.at[some], terms_ref.at[some], sems.at[2 + g])
        )
    for copy in copies[2:] + copies[:2]:
        copy.start()
    out_ref[...] = jnp.zeros_like(out_ref)

    def add(s, carry):
        out_ref[ids_ref[s]] += terms_ref[s].astype(f32)
        return carry

    for g in range(collect_groups):
        copies[2 + g].wait()
        lax.fori_loop(g * group, (g + 1) * group, add, 0, unroll=4)
    for copy in copies[:2]:
        copy.wait()


def body(queries, passages, table, neg_blocks, block_lists, block_counts, pos_index):
    n = lax.axis_size("enc")
    m = lax.axis_size("pb")
    query_rows = queries[0]
    count, width = query_rows.shape
    blocks = table.shape[1]
    pieces = 2 * width // lanes
    per_row = chips_x * cores
    cut_width = width // (2 * ring_cuts)
    table_rows = (
        table[0]
        .reshape(blocks, 2, width // lanes, lanes)
        .transpose(0, 2, 1, 3)
        .reshape(blocks, pieces, lanes)
    )
    whole = pl.BlockSpec(memory_space=pltpu.VMEM)
    in_hbm = pl.BlockSpec(memory_space=pltpu.HBM)
    anywhere = pl.BlockSpec(memory_space=pl.ANY)
    losses, passage_grads, terms, ids = pl.pallas_call(
        functools.partial(exchange_kernel, n, m),
        out_shape=(
            jax.ShapeDtypeStruct((1, count), f32),
            jax.ShapeDtypeStruct((8, width), f32),
            jax.ShapeDtypeStruct((n, pieces, lanes), bf16),
            jax.ShapeDtypeStruct((n,), jnp.int32),
        ),
        in_specs=[in_hbm] * 7,
        out_specs=(whole, whole, anywhere, pl.BlockSpec(memory_space=pltpu.SMEM)),
        scratch_shapes=[
            pltpu.VMEM((count, width), bf16),
            pltpu.VMEM((8, width), bf16),
            pltpu.VMEM((blocks, pieces, lanes), bf16),
            pltpu.VMEM((neg_blocks.shape[2], count), jnp.int32),
            pltpu.VMEM((1, n), jnp.int32),
            pltpu.VMEM((1, count), jnp.int32),
            pltpu.VMEM((n // per_row, 1, n), jnp.int32),
            pltpu.VMEM((per_row, n // per_row, 1, n), jnp.int32),
            pltpu.VMEM((2, 1, n), jnp.int32),
            pltpu.SMEM((2, 1, n), jnp.int32),
            pltpu.VMEM((n, pieces, lanes), bf16),
            pltpu.VMEM((n, pieces, lanes), bf16),
            pltpu.VMEM((n * pieces, lanes), f32),
            pltpu.VMEM((2 * n, width), bf16),
            pltpu.VMEM((ring_cuts, m, 16, cut_width), bf16),
            pltpu.VMEM((2 * n, count), bf16),
            pltpu.VMEM((8 * m, count), bf16),
            pltpu.VMEM((ring_cuts, m, 16, cut_width), f32),
            pltpu.VMEM((n, pieces, lanes), bf16),
            pltpu.VMEM((2, ring_cuts, m // 2, 16, cut_width), bf16),
            pltpu.VMEM((2, ring_cuts, m // 2, 16, cut_width), bf16),
            pltpu.SemaphoreType.DMA((9,)),
            pltpu.SemaphoreType.DMA((4,)),
            pltpu.SemaphoreType.DMA((5,)),
            pltpu.SemaphoreType.DMA((2,)),
            pltpu.SemaphoreType.DMA((2, ring_cuts, m // 2)),
            pltpu.SemaphoreType.DMA((2, ring_cuts, m // 2)),
            pltpu.SemaphoreType.DMA((2, ring_cuts, m // 2)),
            pltpu.SemaphoreType.DMA((2, ring_cuts, m // 2)),
        ],
        compiler_params=pltpu.CompilerParams(
            collective_id=0, has_side_effects=True, vmem_limit_bytes=60 << 20
        ),
        name="exchange",
    )(
        query_rows,
        passages[0],
        table_rows,
        neg_blocks[0].T,
        block_lists[0, 0].reshape(1, n),
        block_counts[0],
        pos_index,
    )
    table_grads, losses, passage_grads = pl.pallas_call(
        collect_kernel,
        out_shape=(
            jax.ShapeDtypeStruct((blocks, pieces, lanes), f32),
            jax.ShapeDtypeStruct((1, count), f32),
            jax.ShapeDtypeStruct((8, width), f32),
        ),
        in_specs=[
            pl.BlockSpec(memory_space=pltpu.SMEM),
            anywhere,
            anywhere,
            anywhere,
        ],
        out_specs=(whole, whole, whole),
        scratch_shapes=[
            pltpu.VMEM((n, pieces, lanes), bf16),
            pltpu.SemaphoreType.DMA((2 + collect_groups,)),
        ],
        compiler_params=pltpu.CompilerParams(vmem_limit_bytes=60 << 20),
        name="collect",
    )(ids, terms, losses, passage_grads)
    table_grads = (
        table_grads.reshape(blocks, width // lanes, 2, lanes)
        .transpose(0, 2, 1, 3)
        .reshape(1, blocks, 2, width)
    )
    return (losses, passage_grads[None], table_grads)


def solution(mesh):
    in_specs = (
        P("enc", "pb", None),
        P("enc", "pb", None),
        P("pb", "enc", None, None),
        P("enc", "pb", None),
        P("enc", "pb", None, None),
        P("enc", "pb", None),
        P("enc", "pb"),
    )
    out_specs = (P("enc", "pb"), P("enc", "pb", None), P("pb", "enc", None, None))
    return jax.shard_map(body, mesh=mesh, in_specs=in_specs, out_specs=out_specs, check_vma=False)
```

time: 102 us -> 93.3 us (0.915)
  local copies, waits for them, and re-layouts: 7.2 us -> 0 us
  Pallas kernels: 93.8 us -> 92.4 us
    unnamed x16 -> x0, local copies, waits for them, and re-layouts: 7.2 us -> none
    pallas_call x1, Pallas kernels: 91.7 us -> 89.4 us  [body(): pl.pallas_call(functools.partial(exchange_kernel, n, m), out_shape=(jax.S...]
where the time goes in v2:
time: 93.3 us; the launch traced here: 93.1 us
  Pallas kernels  92.4 us (99%)
    pallas_call x1, Pallas kernels, body(): pl.pallas_call(functools.partial(exchange_kernel, n, m), out_shape=(jax.S...  89.4 us
    pallas_call x1, Pallas kernels, body(): pl.pallas_call(collect_kernel, out_shape=(jax.ShapeDtypeStruct((blocks, p...  2.99 us

profile of v2, /device:TPU:6, one launch (start us, length us, event | category | flops | bytes accessed | tf_op | source)
XLA Modules:
  0.0 93.1 jit_solution(15796025349623088005)
XLA Ops:
  0.6 89.4 %exchange.1 = (f32[1,192]{1,0:T(1,128)}, f32[8,4096]{1,0:T(8,128)}, bf16[64,64,128]{2,1,0:T(8,128)(2,1)}, s32[64]{0:T(128)}) custom-call(bf16[192,4096]{1,0:T(8,128)(2,1)} %bitcast.18, bf16[8,4096]{1,0:T(8,128)(2,1)} %bitcast.20, bf16[32,64,128]{2,1,0:T(8,128)(2,1)} %bitcast.19, s32[16,192]{1,0:T(8,128)} %bitcast.21, s32[1,64]{1,0:T(1,128)} %bitcast.22, ...), custom_call_target="tpu_custom_call" | custom-call | tf_op jit(solution)/shard_map/exchange/pallas_call | solution.py:445
  90.1 3.0 %collect.1 = (f32[32,64,128]{2,1,0:T(8,128)}, f32[1,192]{1,0:T(1,128)}, f32[8,4096]{1,0:T(8,128)}) custom-call(s32[64]{0:T(128)} %get-tuple-element.10.ids_ref, bf16[64,64,128]{2,1,0:T(8,128)(2,1)} %get-tuple-element.11.terms_hbm, f32[1,192]{1,0:T(1,128)} %get-tuple-element.12.losses_ref, f32[8,4096]{1,0:T(8,128)} %get-tuple-element.13.pgrad_ref), custom_call_target="tpu_custom_call" | custom-call | tf_op jit(solution)/shard_map/collect/pallas_call | solution.py:499

commit v3 on v2

--- a/solution.py
+++ b/solution.py
@@ -93,6 +93,7 @@
     down = lax.rem(z + m - 1, m)
     pieces = fetched.shape[1]
     groups = pieces // 2
+    pitch = pieces + 8
     width = q_v.shape[1]
     cut_width = pg.shape[3]
     per_row = chips_x * cores
@@ -275,7 +276,7 @@
 
     def widen(s, carry):
         origin = source(e, s, n)
-        at = pl.ds(pl.multiple_of(origin * pieces, pieces), pieces)
+        at = pl.ds(pl.multiple_of(origin * pitch, 8), pieces)
         wide[at, :] = fetched[origin].astype(f32)
         return carry
 
@@ -285,7 +286,7 @@
         pltpu.make_async_copy(arrived, arrived, f_sems.at[1 + t]).wait()
         lax.fori_loop(t * quarter, (t + 1) * quarter, widen, 0, unroll=4)
     for j in range(groups):
-        both = [wide[pl.ds(2 * j + r, n, pieces), :] for r in range(2)]
+        both = [wide[pl.ds(2 * j + r, n, pitch), :] for r in range(2)]
         hard[:, j * lanes : (j + 1) * lanes] = jnp.concatenate(both, axis=0).astype(bf16)
     hard_logits = (
         lax.dot_general(hard[...], q_v[...], contract_last, preferred_element_type=f32)
@@ -315,13 +316,13 @@
         )
         for k in range(4):
             for r in range(2):
-                wide[pl.ds(2 * (4 * c + k) + r, n, pieces), :] = part[
+                wide[pl.ds(2 * (4 * c + k) + r, n, pitch), :] = part[
                     r * n : (r + 1) * n, k * lanes : (k + 1) * lanes
                 ]
 
     def give(s, carry):
         peer = partner(e, s, n)
-        tsend[peer] = wide[pl.ds(pl.multiple_of(peer * pieces, pieces), pieces), :].astype(bf16)
+        tsend[peer] = wide[pl.ds(pl.multiple_of(peer * pitch, 8), pieces), :].astype(bf16)
         pltpu.make_async_remote_copy(
             src_ref=tsend.at[peer],
             dst_ref=terms_ref.at[e],
@@ -330,10 +331,6 @@
             device_id={"enc": peer},
         ).start()
         return carry
-
-    lax.fori_loop(1, send_group, give, 0)
-    tsend[e] = wide[pl.ds(pl.multiple_of(e * pieces, pieces), pieces), :].astype(bf16)
-    pltpu.make_async_copy(tsend.at[e], terms_ref.at[e], t_sems.at[1]).start()
 
     for c in range(width // span):
         part = jnp.dot(
@@ -365,8 +362,13 @@
                 rs_send[side, u, t] = held.astype(bf16)
                 carry_on(side, u, t).start()
 
+    reduce_step(0)
+    lax.fori_loop(1, send_group, give, 0)
+    tsend[e] = wide[pl.ds(pl.multiple_of(e * pitch, 8), pieces), :].astype(bf16)
+    pltpu.make_async_copy(tsend.at[e], terms_ref.at[e], t_sems.at[1]).start()
+
     for t in range(max(fwd, n // send_group)):
-        if t < fwd:
+        if 0 < t < fwd:
             reduce_step(t)
         if t > 0 and t * send_group < n:
             lax.fori_loop(t * send_group, min(n, (t + 1) * send_group), give, 0)
@@ -465,7 +467,7 @@
             pltpu.SMEM((2, 1, n), jnp.int32),
             pltpu.VMEM((n, pieces, lanes), bf16),
             pltpu.VMEM((n, pieces, lanes), bf16),
-            pltpu.VMEM((n * pieces, lanes), f32),
+            pltpu.VMEM((n * (pieces + 8), lanes), f32),
             pltpu.VMEM((2 * n, width), bf16),
             pltpu.VMEM((ring_cuts, m, 16, cut_width), bf16),
             pltpu.VMEM((2 * n, count), bf16),

time: 93.3 us -> 90.6 us (0.971)
  Pallas kernels: 92.4 us -> 89.8 us
    pallas_call x1, Pallas kernels: 89.4 us -> 86.8 us  [body(): pl.pallas_call(functools.partial(exchange_kernel, n, m), out_shape=(jax.S...]
where the time goes in v3:
time: 90.6 us; the launch traced here: 90.4 us
  Pallas kernels  89.8 us (99%)
    pallas_call x1, Pallas kernels, body(): pl.pallas_call(functools.partial(exchange_kernel, n, m), out_shape=(jax.S...  86.8 us
    pallas_call x1, Pallas kernels, body(): pl.pallas_call(collect_kernel, out_shape=(jax.ShapeDtypeStruct((blocks, p...  2.98 us

profile of v3, /device:TPU:6, one launch (start us, length us, event | category | flops | bytes accessed | tf_op | source)
XLA Modules:
  0.0 90.4 jit_solution(5639320631299715523)
XLA Ops:
  0.6 86.8 %exchange.1 = (f32[1,192]{1,0:T(1,128)}, f32[8,4096]{1,0:T(8,128)}, bf16[64,64,128]{2,1,0:T(8,128)(2,1)}, s32[64]{0:T(128)}) custom-call(bf16[192,4096]{1,0:T(8,128)(2,1)} %bitcast.18, bf16[8,4096]{1,0:T(8,128)(2,1)} %bitcast.20, bf16[32,64,128]{2,1,0:T(8,128)(2,1)} %bitcast.19, s32[16,192]{1,0:T(8,128)} %bitcast.21, s32[1,64]{1,0:T(1,128)} %bitcast.22, ...), custom_call_target="tpu_custom_call" | custom-call | tf_op jit(solution)/shard_map/exchange/pallas_call | solution.py:447
  87.5 3.0 %collect.1 = (f32[32,64,128]{2,1,0:T(8,128)}, f32[1,192]{1,0:T(1,128)}, f32[8,4096]{1,0:T(8,128)}) custom-call(s32[64]{0:T(128)} %get-tuple-element.10.ids_ref, bf16[64,64,128]{2,1,0:T(8,128)(2,1)} %get-tuple-element.11.terms_hbm, f32[1,192]{1,0:T(1,128)} %get-tuple-element.12.losses_ref, f32[8,4096]{1,0:T(8,128)} %get-tuple-element.13.pgrad_ref), custom_call_target="tpu_custom_call" | custom-call | tf_op jit(solution)/shard_map/collect/pallas_call | solution.py:501

commit v4 on v3

--- a/solution.py
+++ b/solution.py
@@ -235,6 +235,7 @@
     own_wanted = id_scalars[0, 0, row]
     ids_ref[e] = own_wanted
     fetched[e] = table_v[own_wanted]
+    gather_step(0)
     row_part = all_lists.at[pl.ds(0, per_row - 1)]
     pltpu.make_async_copy(row_part, row_part, id_sems.at[3]).wait()
     to_scalars(all_lists[...].reshape(n, n), 1).wait()
@@ -244,8 +245,8 @@
         if t < 4:
             first = max(rows, t * quarter)
             lax.fori_loop(first, (t + 1) * quarter, functools.partial(serve, 1, t), 0)
-        if t < fwd:
-            gather_step(t)
+        if t + 1 < fwd:
+            gather_step(t + 1)
 
     for load in loads[3:]:
         load.wait()

time: 90.6 us -> 91.5 us (level)
  the two profiles are of different devices: /device:TPU:6 before, /device:TPU:1 now
where the time goes in v4:
time: 91.5 us; the launch traced here: 91.3 us
  Pallas kernels  90.7 us (99%)
    pallas_call x1, Pallas kernels, body(): pl.pallas_call(functools.partial(exchange_kernel, n, m), out_shape=(jax.S...  87.7 us
    pallas_call x1, Pallas kernels, body(): pl.pallas_call(collect_kernel, out_shape=(jax.ShapeDtypeStruct((blocks, p...  2.99 us

profile of v4, /device:TPU:1, one launch (start us, length us, event | category | flops | bytes accessed | tf_op | source)
XLA Modules:
  0.0 91.3 jit_solution(15047945001882033957)
XLA Ops:
  0.6 87.7 %exchange.1 = (f32[1,192]{1,0:T(1,128)}, f32[8,4096]{1,0:T(8,128)}, bf16[64,64,128]{2,1,0:T(8,128)(2,1)}, s32[64]{0:T(128)}) custom-call(bf16[192,4096]{1,0:T(8,128)(2,1)} %bitcast.18, bf16[8,4096]{1,0:T(8,128)(2,1)} %bitcast.20, bf16[32,64,128]{2,1,0:T(8,128)(2,1)} %bitcast.19, s32[16,192]{1,0:T(8,128)} %bitcast.21, s32[1,64]{1,0:T(1,128)} %bitcast.22, ...), custom_call_target="tpu_custom_call" | custom-call | tf_op jit(solution)/shard_map/exchange/pallas_call | solution.py:448
  88.3 3.0 %collect.1 = (f32[32,64,128]{2,1,0:T(8,128)}, f32[1,192]{1,0:T(1,128)}, f32[8,4096]{1,0:T(8,128)}) custom-call(s32[64]{0:T(128)} %get-tuple-element.10.ids_ref, bf16[64,64,128]{2,1,0:T(8,128)(2,1)} %get-tuple-element.11.terms_hbm, f32[1,192]{1,0:T(1,128)} %get-tuple-element.12.losses_ref, f32[8,4096]{1,0:T(8,128)} %get-tuple-element.13.pgrad_ref), custom_call_target="tpu_custom_call" | custom-call | tf_op jit(solution)/shard_map/collect/pallas_call | solution.py:502
